TPU v7x, 32 devices: a whole 2x2x4 slice. The times are simulated.
32 devices in a mesh: grp: 2 (over y), vocab: 4 (over x, core), tile: 4 (over z).
Axes of the slice: x: 2, y: 2, z: 4, core: 2. Of those that a mesh axis runs over, the one named last changes fastest.
Arguments:
- embed: bfloat16 [512, 8192], P('vocab', 'tile'), may hold values from -6 to 6
- unembed: bfloat16 [512, 8192], P('vocab', 'tile'), may hold values from -6 to 6
- q_weight: bfloat16 [2, 8192, 4096], P(None, 'tile', 'vocab'), may hold values from -0.0625 to 0.0625
- k_weight: bfloat16 [2, 8192, 512], P(None, 'tile'), may hold values from -0.0625 to 0.0625
- v_weight: bfloat16 [2, 8192, 512], P(None, 'tile'), may hold values from -0.0625 to 0.0625
- o_weight: bfloat16 [2, 4096, 8192], P(None, 'vocab', 'tile'), may hold values from -0.0625 to 0.0625
- offsets: int32 [2], P('grp'), parts along dimension 0, may hold values from 0 to 64
Outputs:
- ov_core: float32 [4, 32, 128, 128], P('grp', 'vocab', 'tile'), parts along dimension 0
- qk_core: float32 [4, 32, 128, 128], P('grp', 'vocab', 'tile'), parts along dimension 0
There are 2 independent parts, one for each index of `grp`. A program takes and returns all parts, laid end to end along the dimension named above; an argument that names none is the same for every part. Nothing has to cross between parts.
All inputs are finite; a program needn't handle non-finite values.
Results may differ from a plain program's by a relative error of at most 0.017.
Values may be sent and summed in bfloat16 or wider, within the bound.
A program may use at most 128 MiB of HBM per device.

v0:
```python
import math

import jax
import jax.numpy as jnp
from jax import lax
from jax.sharding import PartitionSpec as P

HD = 128
GROUP = 8
SLAB_DEV = 64


def pair_panel(stacked):
    return jnp.transpose(stacked, (1, 0, 2)).reshape(stacked.shape[1], -1)


def local(embed, unembed, q_weight, k_weight, v_weight, o_weight, offsets):
    start_row = offsets[0]
    slab_e = lax.dynamic_slice_in_dim(embed, start_row, SLAB_DEV, 0)
    slab_u = lax.dynamic_slice_in_dim(unembed, start_row, SLAB_DEV, 0)
    all_e, all_u = (
        lax.all_gather(slab_e, "vocab", axis=0, tiled=True),
        lax.all_gather(slab_u, "vocab", axis=0, tiled=True),
    )
    layer_count = q_weight.shape[0]
    head_count = q_weight.shape[2] // HD
    kv_start = lax.axis_index("vocab") * head_count // GROUP * HD
    q_panel = pair_panel(q_weight)
    k_panel = pair_panel(lax.dynamic_slice_in_dim(k_weight, kv_start, HD, 2))
    v_panel = pair_panel(lax.dynamic_slice_in_dim(v_weight, kv_start, HD, 2))
    o_panel = o_weight.reshape(-1, o_weight.shape[2])
    q_width = q_panel.shape[1]
    k_width = k_panel.shape[1]
    slab_total = all_e.shape[0]
    scale_factor = 1.0 / math.sqrt(slab_total)
    tile_count = lax.axis_size("tile")
    full_terms = jnp.concatenate(
        [
            jnp.dot(all_e, q_panel, preferred_element_type=jnp.float32),
            jnp.dot(all_e, k_panel, preferred_element_type=jnp.float32),
            jnp.dot(all_e, v_panel, preferred_element_type=jnp.float32),
            lax.dot_general(
                all_u, o_panel, (((1,), (1,)), ((), ())), preferred_element_type=jnp.float32
            ),
        ],
        axis=1,
    )
    q_side = full_terms[:, :q_width]
    k_side = full_terms[:, q_width : q_width + k_width]
    v_side = full_terms[:, q_width + k_width : q_width + 2 * k_width]
    o_side = full_terms[:, q_width + 2 * k_width :]
    q_side, k_side, v_side, o_side = (q_side, k_side, v_side, o_side)
    rows_each = HD // tile_count

    def spread(side):
        shaped = side.reshape(slab_total, layer_count, head_count, tile_count, rows_each)
        return jnp.transpose(shaped, (0, 3, 1, 2, 4)).reshape(slab_total, -1)

    row_q, row_o = (
        lax.psum_scatter(
            spread(q_side).astype(jnp.bfloat16), "tile", scatter_dimension=1, tiled=True
        ).astype(jnp.float32),
        lax.psum_scatter(
            spread(o_side).astype(jnp.bfloat16), "tile", scatter_dimension=1, tiled=True
        ).astype(jnp.float32),
    )
    key_k, key_v = (
        lax.psum(k_side.astype(jnp.bfloat16), "tile").astype(jnp.float32),
        lax.psum(v_side.astype(jnp.bfloat16), "tile").astype(jnp.float32),
    )
    q_heads = row_q.astype(jnp.bfloat16).reshape(slab_total, layer_count, head_count, rows_each)
    o_heads = row_o.astype(jnp.bfloat16).reshape(slab_total, layer_count, head_count, rows_each)
    k_heads = key_k.astype(jnp.bfloat16).reshape(slab_total, layer_count, HD)
    v_heads = key_v.astype(jnp.bfloat16).reshape(slab_total, layer_count, HD)
    qk_core = (
        jnp.einsum("slhr,slc->lhrc", q_heads, k_heads, preferred_element_type=jnp.float32)
        * scale_factor
    )
    ov_core = (
        jnp.einsum("slhr,slc->lhrc", o_heads, v_heads, preferred_element_type=jnp.float32)
        * scale_factor
    )
    return (ov_core, qk_core)


def solution(mesh):
    return jax.shard_map(
        local,
        mesh=mesh,
        in_specs=(
            P("vocab", "tile"),
            P("vocab", "tile"),
            P(None, "tile", "vocab"),
            P(None, "tile", None),
            P(None, "tile", None),
            P(None, "vocab", "tile"),
            P("grp"),
        ),
        out_specs=(P("grp", "vocab", "tile", None), P("grp", "vocab", "tile", None)),
        check_vma=False,
    )
```

profile of v0, /device:TPU:1, one launch (start us, length us, event | category | flops | bytes accessed | tf_op | source)
XLA Modules:
  0.0 151.8 jit_solution(10593856841823776878)
XLA Ops:
  7.9 0.3 copy-done
  8.2 0.8 constant_dynamic-slice_fusion.2
  9.0 0.0 all-gather.3.cloned.1.call-start
  9.1 1.7 %constant_dynamic-slice_fusion.3 = bf16[64,2048]{1,0:T(8,128)(2,1)} fusion(bf16[128,2048]{1,0:T(8,128)(2,1)} %param.8, s32[]{:T(128)S(6)} %select_n.13), kind=kLoop, calls=%fused_computation.15 | loop fusion | bytes 524292 | tf_op jit(solution)/shard_map/dynamic_slice | solution.py:20
  10.9 1.7 %constant_dynamic-slice_fusion = (bf16[2,2048,128]{2,1,0:T(8,128)(2,1)S(1)}, bf16[2,2048,128]{2,1,0:T(8,128)(2,1)S(1)}) fusion(bf16[2,2048,512]{2,1,0:T(8,128)(2,1)} %param.10, s32[]{:T(128)S(6)} %select_n.15, bf16[2,2048,512]{2,1,0:T(8,128)(2,1)} %param.11), kind=kLoop, calls=%fused_computation.12 | loop fusion | bytes 4194308 | tf_op jit(solution)/shard_map/dynamic_slice | solution.py:29
  12.6 1.3 copy.22
  13.9 0.5 copy.23
  14.5 11.8 %copy.14 = bf16[2,2048,1024]{1,2,0:T(8,128)(2,1)} copy(bf16[2,2048,1024]{2,1,0:T(8,128)(2,1)} %param.9) | data formatting | bytes 16777216 | tf_op args[2]
  26.3 3.1 %all-gather.5.cloned.1.call-done = bf16[256,2048]{1,0:T(8,128)(2,1)} async-done(((bf16[64,2048]{1,0:T(8,128)(2,1)}), bf16[256,2048]{1,0:T(8,128)(2,1)}) %all-gather.5.cloned.1.call-update) | async-done | bytes 1048592 | tf_op jit(solution)/shard_map/all_gather | solution.py:22
  29.4 1.7 %convolution_convert_fusion.3 = bf16[256,256]{0,1:T(8,128)(2,1)S(1)} fusion(bf16[256,2048]{1,0:T(8,128)(2,1)} %all-gather.5.cloned.1.call-done, bf16[2048,256]{0,1:T(8,128)(2,1)S(1)} %bitcast.60), kind=kOutput, calls=%fused_computation.7 | convolution fusion | flops 268500992 | bytes 2228224 | tf_op jit(solution)/shard_map/dot_general | solution.py:41
  31.1 0.8 copy.13
  31.8 1.7 %convolution_convert_fusion.2 = bf16[256,256]{0,1:T(8,128)(2,1)S(1)} fusion(bf16[256,2048]{1,0:T(8,128)(2,1)} %all-gather.5.cloned.1.call-done, bf16[2048,256]{0,1:T(8,128)(2,1)S(1)} %bitcast.59), kind=kOutput, calls=%fused_computation.6 | convolution fusion | flops 268500992 | bytes 2228224 | tf_op jit(solution)/shard_map/dot_general | solution.py:40
  33.5 0.7 copy.17
  34.3 0.0 reduce-scatter.5.cloned.1.call-start
  34.4 6.2 %fusion.1 = bf16[256,4,2,8,32]{0,4,1,3,2:T(8,128)(2,1)S(1)} fusion(bf16[2,8,4,32,2048]{4,3,2,1,0:T(8,128)(2,1)} %bitcast.56, bf16[256,2048]{1,0:T(8,128)(2,1)} %all-gather.5.cloned.1.call-done), kind=kOutput, calls=%fused_computation.3 | convolution fusion | flops 2148007936 | bytes 10485760 | tf_op jit(solution)/shard_map/dot_general | solution.py:39
  40.5 1.1 copy.15
  41.7 6.6 %all-gather.3.cloned.1.call-done = bf16[256,2048]{1,0:T(8,128)(2,1)} async-done(((bf16[64,2048]{1,0:T(8,128)(2,1)}), bf16[256,2048]{1,0:T(8,128)(2,1)}) %all-gather.3.cloned.1.call-update) | async-done | bytes 1048592 | tf_op jit(solution)/shard_map/all_gather | solution.py:23
  48.3 6.1 %fusion = bf16[256,4,2,8,32]{0,4,1,3,2:T(8,128)(2,1)S(1)} fusion(bf16[2,8,4,32,2048]{4,3,2,1,0:T(8,128)(2,1)} %bitcast.65, bf16[256,2048]{1,0:T(8,128)(2,1)} %all-gather.3.cloned.1.call-done), kind=kOutput, calls=%fused_computation.2 | convolution fusion | flops 2148007936 | bytes 10485760 | tf_op jit(solution)/shard_map/dot_general | solution.py:42
  54.4 1.1 copy.11
  55.5 29.4 %all-reduce.3.cloned.1.call-done = (bf16[256,2,128]{2,0,1:T(8,128)(2,1)}, bf16[256,2,128]{2,0,1:T(8,128)(2,1)}) async-done(((bf16[256,2,128]{2,0,1:T(8,128)(2,1)}, bf16[256,2,128]{2,0,1:T(8,128)(2,1)}), (bf16[256,2,128]{2,0,1:T(8,128)(2,1)}, bf16[256,2,128]{2,0,1:T(8,128)(2,1)})) %all-reduce.3.cloned.1.call-update) | async-done | bytes 262160 | tf_op jit(solution)/shard_map/psum | solution.py:69
  84.9 30.5 %reduce-scatter.5.cloned.1.call-done = bf16[256,512]{0,1:T(8,128)(2,1)} async-done(((bf16[256,2048]{0,1:T(8,128)(2,1)}), bf16[256,512]{0,1:T(8,128)(2,1)}) %reduce-scatter.5.cloned.1.call-update) | async-done | bytes 262160 | tf_op jit(solution)/shard_map/reduce_scatter | solution.py:60
  115.4 1.9 %convolution_multiply_fusion = f32[2,8,32,128]{3,2,1,0:T(8,128)} fusion(bf16[256,2,8,32]{0,3,2,1:T(8,128)(2,1)} %bitcast.63, bf16[256,2,128]{2,0,1:T(8,128)(2,1)} %get-tuple-element.3), kind=kOutput, calls=%fused_computation.4 | convolution fusion | flops 33619968 | bytes 655360 | tf_op jit(solution)/shard_map/slhr,slc->lhrc/dot_general | solution.py:76
  117.3 26.0 %reduce-scatter.3.cloned.1.call-done = bf16[256,512]{0,1:T(8,128)(2,1)} async-done(((bf16[256,2048]{0,1:T(8,128)(2,1)}), bf16[256,512]{0,1:T(8,128)(2,1)}) %reduce-scatter.3.cloned.1.call-update) | async-done | bytes 262160 | tf_op jit(solution)/shard_map/reduce_scatter | solution.py:63
  143.4 1.9 %convolution_multiply_fusion.1 = f32[2,8,32,128]{3,2,1,0:T(8,128)} fusion(bf16[256,2,8,32]{0,3,2,1:T(8,128)(2,1)} %bitcast.64, bf16[256,2,128]{2,0,1:T(8,128)(2,1)} %get-tuple-element.2), kind=kOutput, calls=%fused_computation.5 | convolution fusion | flops 33619968 | bytes 655360 | tf_op jit(solution)/shard_map/slhr,slc->lhrc/dot_general | solution.py:80
  (11 shorter events, 0.2 us)
Async XLA Ops:
  7.2 1.1 copy-start
  7.2 22.2 %all-gather.5.cloned.1.call-start = ((), (), s32[]{:S(2)}) async-start(), calls=%async_computation.4 | async-start | bytes 1310720 | tf_op jit(solution)/shard_map/all_gather | solution.py:22
  9.0 39.3 %all-gather.3.cloned.1.call-start = ((), (), s32[]{:S(2)}) async-start(), calls=%async_computation.2 | async-start | bytes 1310720 | tf_op jit(solution)/shard_map/all_gather | solution.py:23
  10.8 74.1 %all-reduce.3.cloned.1.call-start = ((), (), s32[]{:S(2)}) async-start(), calls=%async_computation.6 | async-start | bytes 524288 | tf_op jit(solution)/shard_map/psum | solution.py:69
  14.5 14.9 %copy-start.1 = (bf16[2,2048,128]{1,2,0:T(8,128)(2,1)S(1)}, bf16[2,2048,128]{1,2,0:T(8,128)(2,1)}, u32[]{:S(2)}) copy-start(bf16[2,2048,128]{1,2,0:T(8,128)(2,1)} %copy.22) | copy-start | bytes 3145732
  34.3 81.1 %reduce-scatter.5.cloned.1.call-start = ((), (), s32[]{:S(2)}) async-start(), calls=%async_computation.5 | async-start | bytes 1310720 | tf_op jit(solution)/shard_map/reduce_scatter | solution.py:60
  41.7 101.7 %reduce-scatter.3.cloned.1.call-start = ((), (), s32[]{:S(2)}) async-start(), calls=%async_computation.3 | async-start | bytes 1310720 | tf_op jit(solution)/shard_map/reduce_scatter | solution.py:63
Sparse Core Ops, SparseCore 0:
  10.1 19.1 all-gather.4
  31.5 16.7 all-gather.2
  51.2 33.6 all-reduce.2
  87.1 28.2 reduce-scatter.4
  117.6 25.7 reduce-scatter.2
where the time goes:
time: 153 us; the launch traced here: 152 us
  waiting for transfers between devices  95.7 us (63%)
  local copies, waits for them, and re-layouts  21.9 us (14%)
  matrix products  19.5 us (13%)
  between operations  14.6 us (10%)
    reduce_scatter x1, waiting for transfers between devices, local(): lax.psum_scatter(spread(q_side).astype(jnp.bfloat16), 'tile', scatter_dim...  30.5 us
    psum x1, waiting for transfers between devices, local(): lax.psum(v_side.astype(jnp.bfloat16), 'tile').astype(jnp.float32)  29.4 us
    reduce_scatter x1, waiting for transfers between devices, local(): lax.psum_scatter(spread(o_side).astype(jnp.bfloat16), 'tile', scatter_dim...  26 us
    unnamed x7, local copies, waits for them, and re-layouts  14 us
    all_gather x1, waiting for transfers between devices, local(): lax.all_gather(slab_u, 'vocab', axis=0, tiled=True)  6.56 us
    dot_general x1, matrix products, local(): jnp.dot(all_e, q_panel, preferred_element_type=jnp.float32)  6.17 us
    dot_general x1, matrix products, local(): lax.dot_general(all_u, o_panel, (((1,), (1,)), ((), ())), preferred_eleme...  6.1 us
    all_gather x1, waiting for transfers between devices, local(): lax.all_gather(slab_e, 'vocab', axis=0, tiled=True)  3.08 us
  transfers between devices with their start and end apart: 5, of which 5 were waited for; matrix products, arithmetic and copies ran while one was open for 25% of the time, Pallas kernels for 0%

commit v1 on v0

v1 whole, which is shorter than its diff:
```python
import math

import jax
import jax.numpy as jnp
from jax import lax
from jax.sharding import PartitionSpec as P

HD = 128
GROUP = 8
SLAB_DEV = 64


def local(embed, unembed, q_weight, k_weight, v_weight, o_weight, offsets):
    start_row = offsets[0]
    slab_e = lax.dynamic_slice_in_dim(embed, start_row, SLAB_DEV, 0)
    slab_u = lax.dynamic_slice_in_dim(unembed, start_row, SLAB_DEV, 0)
    all_e = lax.all_gather(slab_e, "vocab", axis=0, tiled=True)
    all_u = lax.all_gather(slab_u, "vocab", axis=0, tiled=True)
    layers = q_weight.shape[0]
    heads = q_weight.shape[2] // HD
    kv_start = lax.axis_index("vocab") * heads // GROUP * HD
    k_panel = lax.dynamic_slice_in_dim(k_weight, kv_start, HD, 2)
    v_panel = lax.dynamic_slice_in_dim(v_weight, kv_start, HD, 2)
    scale = 1.0 / math.sqrt(all_e.shape[0])
    tiles = lax.axis_size("tile")
    rows_each = HD // tiles
    bf16, f32 = jnp.bfloat16, jnp.float32

    k_part = jnp.einsum("sd,ldc->lsc", all_e, k_panel, preferred_element_type=f32).astype(bf16)
    v_part = jnp.einsum("sd,ldc->lsc", all_e, v_panel, preferred_element_type=f32).astype(bf16)
    k_side, v_side = lax.psum((k_part, v_part), "tile")
    k_wide = jnp.einsum("lsc,sd->lcd", k_side, all_e, preferred_element_type=f32).astype(bf16)
    v_wide = jnp.einsum("lsc,sd->lcd", v_side, all_u, preferred_element_type=f32).astype(bf16)
    qk = jnp.einsum("ldr,lcd->lrc", q_weight, k_wide, preferred_element_type=f32)
    ov = jnp.einsum("lrd,lcd->lrc", o_weight, v_wide, preferred_element_type=f32)

    def finish(part):
        part = (part * scale).astype(bf16).reshape(layers, heads, tiles, rows_each, HD)
        part = jnp.transpose(part, (2, 0, 1, 3, 4)).reshape(tiles * layers * heads * rows_each, HD)
        mine = lax.psum_scatter(part, "tile", scatter_dimension=0, tiled=True)
        return mine.reshape(layers, heads, rows_each, HD).astype(f32)

    return finish(ov), finish(qk)


def solution(mesh):
    return jax.shard_map(
        local,
        mesh=mesh,
        in_specs=(
            P("vocab", "tile"),
            P("vocab", "tile"),
            P(None, "tile", "vocab"),
            P(None, "tile", None),
            P(None, "tile", None),
            P(None, "vocab", "tile"),
            P("grp"),
        ),
        out_specs=(P("grp", "vocab", "tile", None), P("grp", "vocab", "tile", None)),
        check_vma=False,
    )
```

time: 153 us -> 144 us (0.941)
  local copies, waits for them, and re-layouts: 21.9 us -> 5.1 us
  waiting for transfers between devices: 95.7 us -> 101 us
  other arithmetic: 0 us -> 3.26 us
  matrix products: 19.5 us -> 17.6 us
    all_gather x2, waiting for transfers between devices: 9.64 us -> 34.4 us  [the longest x1 20.3 us: local(): all_e = lax.all_gather(slab_e, 'vocab', axis=0, tiled=True)]
    reduce_scatter x2, waiting for transfers between devices: 56.6 us -> 34.3 us  [finish(): mine = lax.psum_scatter(part, 'tile', scatter_dimension=0, tiled=True)]
    unnamed x7 -> x4, local copies, waits for them, and re-layouts: 14 us -> 0.31 us
    convert_element_type x0 -> x2, other arithmetic: none -> 3.26 us  [finish(): return mine.reshape(layers, heads, rows_each, HD).astype(f32)]
    psum x1, waiting for transfers between devices: 29.4 us -> 31.9 us  [local(): k_side, v_side = lax.psum((k_part, v_part), 'tile')]
    dot_general x6 -> x4, matrix products: 19.5 us -> 17.6 us  [the longest x1 6.85 us: local(): jnp.einsum('lrd,lcd->lrc', o_weight, v_wide, preferred_element_type=f32)]
    transpose x0 -> x2, local copies, waits for them, and re-layouts: none -> 1.74 us  [finish(): jnp.transpose(part, (2, 0, 1, 3, 4))]
    dynamic_slice x1 -> x0, local copies, waits for them, and re-layouts: 1.72 us -> none  [local(): k_panel = pair_panel(lax.dynamic_slice_in_dim(k_weight, kv_start, HD, 2))]
  transfers between devices with their start and end apart: 5 -> 5, of which waited for: 5 -> 5; matrix products, arithmetic and copies ran while one was open for 25% -> 13% of each run, Pallas kernels for 0% -> 0%
where the time goes in v1:
time: 144 us; the launch traced here: 141 us
  waiting for transfers between devices  101 us (70%)
  matrix products  17.6 us (12%)
  between operations  14.5 us (10%)
  local copies, waits for them, and re-layouts  5.1 us (4%)
  other arithmetic  3.26 us (2%)
    reduce_scatter x2, waiting for transfers between devices, finish(): mine = lax.psum_scatter(part, 'tile', scatter_dimension=0, tiled=True)  34.3 us
    psum x1, waiting for transfers between devices, local(): k_side, v_side = lax.psum((k_part, v_part), 'tile')  31.9 us
    all_gather x1, waiting for transfers between devices, local(): all_e = lax.all_gather(slab_e, 'vocab', axis=0, tiled=True)  20.3 us
    all_gather x1, waiting for transfers between devices, local(): all_u = lax.all_gather(slab_u, 'vocab', axis=0, tiled=True)  14.1 us
    dot_general x1, matrix products, local(): jnp.einsum('lrd,lcd->lrc', o_weight, v_wide, preferred_element_type=f32)  6.85 us
    dot_general x1, matrix products, local(): jnp.einsum('ldr,lcd->lrc', q_weight, k_wide, preferred_element_type=f32)  5.33 us
    convert_element_type x2, other arithmetic, finish(): return mine.reshape(layers, heads, rows_each, HD).astype(f32)  3.26 us
  transfers between devices with their start and end apart: 5, of which 5 were waited for; matrix products, arithmetic and copies ran while one was open for 13% of the time, Pallas kernels for 0%

profile of v1, /device:TPU:1, one launch (start us, length us, event | category | flops | bytes accessed | tf_op | source)
XLA Modules:
  0.0 141.4 jit_solution(2450073788664595228)
XLA Ops:
  7.2 0.0 all-gather.3.cloned.1.call-start
  7.9 0.3 copy-done
  8.2 0.8 constant_dynamic-slice_fusion.1
  9.0 0.0 all-gather.3.cloned.1.call-update
  9.0 0.0 all-reduce.3.cloned.1.call-start
  9.1 20.3 %all-gather.3.cloned.1.call-done = bf16[256,2048]{1,0:T(8,128)(2,1)} async-done(((bf16[64,2048]{1,0:T(8,128)(2,1)}), bf16[256,2048]{1,0:T(8,128)(2,1)}) %all-gather.3.cloned.1.call-update) | async-done | bytes 1048592 | tf_op jit(solution)/shard_map/all_gather | solution.py:17
  29.4 2.7 %fusion.5 = bf16[2,256,128]{1,2,0:T(8,128)(2,1)} fusion(bf16[256,2048]{1,0:T(8,128)(2,1)} %all-gather.3.cloned.1.call-done, bf16[2,2048,512]{2,1,0:T(8,128)(2,1)} %param.10, s32[]{:T(128)S(6)} %select_n.14), kind=kOutput, calls=%fused_computation.11 | convolution fusion | flops 268500992 | bytes 2228228 | tf_op jit(solution)/shard_map/sd,ldc->lsc/dot_general | solution.py:29
  32.1 2.7 %fusion.4 = bf16[2,256,128]{1,2,0:T(8,128)(2,1)} fusion(bf16[256,2048]{1,0:T(8,128)(2,1)} %all-gather.3.cloned.1.call-done, bf16[2,2048,512]{2,1,0:T(8,128)(2,1)} %param.11, s32[]{:T(128)S(6)} %select_n.14), kind=kOutput, calls=%fused_computation.10 | convolution fusion | flops 268500992 | bytes 2228228 | tf_op jit(solution)/shard_map/sd,ldc->lsc/dot_general | solution.py:30
  34.8 0.0 all-gather.5.cloned.1.call-start
  34.9 1.7 %constant_dynamic-slice_fusion = bf16[64,2048]{1,0:T(8,128)(2,1)} fusion(bf16[128,2048]{1,0:T(8,128)(2,1)} %param.8, s32[]{:T(128)S(6)} %select_n.15), kind=kLoop, calls=%fused_computation.19 | loop fusion | bytes 524292 | tf_op jit(solution)/shard_map/dynamic_slice | solution.py:16
  36.6 0.0 reduce-scatter.5.cloned.1.call-start
  36.7 31.9 %all-reduce.3.cloned.1.call-done = (bf16[2,256,128]{1,2,0:T(8,128)(2,1)}, bf16[2,256,128]{1,2,0:T(8,128)(2,1)}) async-done(((bf16[2,256,128]{1,2,0:T(8,128)(2,1)}, bf16[2,256,128]{1,2,0:T(8,128)(2,1)}), (bf16[2,256,128]{1,2,0:T(8,128)(2,1)}, bf16[2,256,128]{1,2,0:T(8,128)(2,1)})) %all-reduce.3.cloned.1.call-update) | async-done | bytes 262160 | tf_op jit(solution)/shard_map/psum | solution.py:31
  68.6 5.3 %fusion.2 = bf16[2,1024,128]{1,2,0:T(8,128)(2,1)S(1)} fusion(bf16[2,2048,1024]{2,1,0:T(8,128)(2,1)} %param.9, bf16[2,256,128]{1,2,0:T(8,128)(2,1)} %get-tuple-element.3, bf16[256,2048]{1,0:T(8,128)(2,1)} %all-gather.3.cloned.1.call-done), kind=kOutput, calls=%fused_computation.6 | convolution fusion | flops 1343225856 | bytes 10092544 | tf_op jit(solution)/shard_map/ldr,lcd->lrc/dot_general | solution.py:34
  74.0 0.3 copy.11
  74.2 0.9 copy.12
  75.2 0.0 reduce-scatter.3.cloned.1.call-start
  75.2 14.1 %all-gather.5.cloned.1.call-done = bf16[256,2048]{1,0:T(8,128)(2,1)} async-done(((bf16[64,2048]{1,0:T(8,128)(2,1)}), bf16[256,2048]{1,0:T(8,128)(2,1)}) %all-gather.5.cloned.1.call-update) | async-done | bytes 1048592 | tf_op jit(solution)/shard_map/all_gather | solution.py:18
  89.3 6.9 %fusion.3 = bf16[2,1024,128]{1,2,0:T(8,128)(2,1)S(1)} fusion(bf16[2,1024,2048]{2,1,0:T(8,128)(2,1)} %param.12, bf16[2,256,128]{1,2,0:T(8,128)(2,1)S(1)} %copy-done.1, bf16[256,2048]{1,0:T(8,128)(2,1)} %all-gather.5.cloned.1.call-done), kind=kOutput, calls=%fused_computation.7 | convolution fusion | flops 1343225856 | bytes 10092544 | tf_op jit(solution)/shard_map/lrd,lcd->lrc/dot_general | solution.py:35
  96.1 0.3 copy.9
  96.4 0.8 copy.10
  97.3 13.8 %reduce-scatter.5.cloned.1.call-done = bf16[512,128]{1,0:T(8,128)(2,1)} async-done(((bf16[2048,128]{1,0:T(8,128)(2,1)}), bf16[512,128]{1,0:T(8,128)(2,1)}) %reduce-scatter.5.cloned.1.call-update) | async-done | bytes 131088 | tf_op jit(solution)/shard_map/reduce_scatter | solution.py:40
  111.1 1.6 %convert.3 = f32[2,8,32,128]{3,2,1,0:T(8,128)} convert(bf16[2,8,32,128]{3,2,1,0:T(8,128)(2,1)} %bitcast.44) | non-fusion elementwise | flops 65536 | bytes 393216 | tf_op jit(solution)/shard_map/convert_element_type | solution.py:41
  112.7 20.5 %reduce-scatter.3.cloned.1.call-done = bf16[512,128]{1,0:T(8,128)(2,1)} async-done(((bf16[2048,128]{1,0:T(8,128)(2,1)}), bf16[512,128]{1,0:T(8,128)(2,1)}) %reduce-scatter.3.cloned.1.call-update) | async-done | bytes 131088 | tf_op jit(solution)/shard_map/reduce_scatter | solution.py:40
  133.2 1.6 %convert.2 = f32[2,8,32,128]{3,2,1,0:T(8,128)} convert(bf16[2,8,32,128]{3,2,1,0:T(8,128)(2,1)} %bitcast.45) | non-fusion elementwise | flops 65536 | bytes 393216 | tf_op jit(solution)/shard_map/convert_element_type | solution.py:41
  (7 shorter events, 0.1 us)
Async XLA Ops:
  7.2 1.1 copy-start
  7.2 22.2 %all-gather.3.cloned.1.call-start = ((), (), s32[]{:S(2)}) async-start(), calls=%async_computation.2 | async-start | bytes 1310720 | tf_op jit(solution)/shard_map/all_gather | solution.py:17
  9.0 59.6 %all-reduce.3.cloned.1.call-start = ((), (), s32[]{:S(2)}) async-start(), calls=%async_computation.6 | async-start | bytes 524288 | tf_op jit(solution)/shard_map/psum | solution.py:31
  34.8 54.5 %all-gather.5.cloned.1.call-start = ((), (), s32[]{:S(2)}) async-start(), calls=%async_computation.3 | async-start | bytes 1310720 | tf_op jit(solution)/shard_map/all_gather | solution.py:18
  36.6 74.4 %reduce-scatter.5.cloned.1.call-start = ((), (), s32[]{:S(2)}) async-start(), calls=%async_computation.5 | async-start | bytes 655360 | tf_op jit(solution)/shard_map/reduce_scatter | solution.py:40
  68.6 20.6 %copy-start.1 = (bf16[2,256,128]{1,2,0:T(8,128)(2,1)S(1)}, bf16[2,256,128]{1,2,0:T(8,128)(2,1)}, u32[]{:S(2)}) copy-start(bf16[2,256,128]{1,2,0:T(8,128)(2,1)} %get-tuple-element.2) | copy-start | bytes 393220
  75.2 58.0 %reduce-scatter.3.cloned.1.call-start = ((), (), s32[]{:S(2)}) async-start(), calls=%async_computation.4 | async-start | bytes 655360 | tf_op jit(solution)/shard_map/reduce_scatter | solution.py:40
Sparse Core Ops, SparseCore 0:
  10.1 19.1 all-gather.2
  34.9 33.6 all-reduce.2
  70.8 18.3 all-gather.4
  91.5 19.5 reduce-scatter.4
  113.3 19.8 reduce-scatter.2

commit v2 on v1

v2 whole, which is shorter than its diff:
```python
import functools
import math

import jax
import jax.numpy as jnp
from jax import lax
from jax.experimental import pallas as pl
from jax.experimental.pallas import tpu as pltpu
from jax.sharding import PartitionSpec as P

HD = 128
GROUP = 8
SLAB_DEV = 64
MESH = pl.DeviceIdType.MESH
BF16, F32 = jnp.bfloat16, jnp.float32


def kernel(nv, nt, layers, heads, off_ref, e_hbm, u_hbm, q_hbm, k_hbm, v_hbm, o_hbm,
           ov_ref, qk_ref, e_raw, u_raw, e_all, u_all, q_w, o_w, kv_w, part, rs_in, kv_all,
           wide, c_out, c_in, raw_sem, w_sem, e_send, e_recv, u_send, u_recv,
           rs_send, rs_recv, ag_send, ag_recv, c_send, c_recv):
    vme, tme = lax.axis_index("vocab"), lax.axis_index("tile")
    v_to = [lax.rem(vme + d, nv) for d in range(nv)]
    t_to = [lax.rem(tme + d, nt) for d in range(nt)]
    t_from = [lax.rem(tme + nt - d, nt) for d in range(nt)]
    depth = e_raw.shape[1]
    rows = nv * SLAB_DEV
    chunk = rows // nt
    each = HD // nt

    barrier = pltpu.get_barrier_semaphore()
    for d in range(1, nv):
        pl.semaphore_signal(barrier, inc=1, device_id={"vocab": v_to[d]}, device_id_type=MESH)
    for d in range(1, nt):
        pl.semaphore_signal(barrier, inc=1, device_id={"tile": t_to[d]}, device_id_type=MESH)

    raw = [pltpu.make_async_copy(e_hbm, e_raw, raw_sem.at[0]),
           pltpu.make_async_copy(u_hbm, u_raw, raw_sem.at[1])]
    for copy in raw:
        copy.start()
    start = pl.multiple_of(vme * heads // GROUP * HD, HD)
    kv_loads = []
    for l in range(layers):
        for kind, src in enumerate((k_hbm, v_hbm)):
            kv_loads.append(pltpu.make_async_copy(
                src.at[l, :, pl.ds(start, HD)],
                kv_w.at[l, :, pl.ds(kind * HD, HD)], w_sem.at[2 * l + kind]))
    big_loads = []
    for kind, (src, dst) in enumerate(((q_hbm, q_w), (o_hbm, o_w))):
        for l in range(layers):
            big_loads.append(pltpu.make_async_copy(
                src.at[l], dst.at[l], w_sem.at[2 * layers + kind * layers + l]))

    off = off_ref[0]
    row = lax.broadcasted_iota(jnp.int32, (SLAB_DEV, e_raw.shape[0]), 0)
    col = lax.broadcasted_iota(jnp.int32, (SLAB_DEV, e_raw.shape[0]), 1)
    pick = jnp.where(col == row + off, 1.0, 0.0).astype(BF16)
    raw[0].wait()
    e_all[:SLAB_DEV] = jnp.dot(pick, e_raw[...], preferred_element_type=F32).astype(BF16)
    raw[1].wait()
    u_all[:SLAB_DEV] = jnp.dot(pick, u_raw[...], preferred_element_type=F32).astype(BF16)
    for copy in kv_loads + big_loads:
        copy.start()

    pl.semaphore_wait(barrier, nv - 1 + nt - 1)

    def to_vocab(buf, d, send, recv):
        return pltpu.make_async_remote_copy(
            src_ref=buf.at[pl.ds(0, SLAB_DEV)], dst_ref=buf.at[pl.ds(d * SLAB_DEV, SLAB_DEV)],
            send_sem=send.at[d], recv_sem=recv.at[d],
            device_id={"vocab": v_to[d]}, device_id_type=MESH)

    e_copies = [to_vocab(e_all, d, e_send, e_recv) for d in range(1, nv)]
    u_copies = [to_vocab(u_all, d, u_send, u_recv) for d in range(1, nv)]
    for copy in e_copies:
        copy.start()
    for copy in u_copies:
        copy.start()

    for copy in kv_loads:
        copy.wait()
    for copy in e_copies:
        copy.wait_recv()
    for l in range(layers):
        got = jnp.dot(e_all[...], kv_w[l], preferred_element_type=F32).astype(BF16)
        for t in range(nt):
            part[t, :, 2 * HD * l:2 * HD * (l + 1)] = got[t * chunk:(t + 1) * chunk]

    rs_copies = [pltpu.make_async_remote_copy(
        src_ref=part.at[t_to[d]], dst_ref=rs_in.at[d], send_sem=rs_send.at[d],
        recv_sem=rs_recv.at[d], device_id={"tile": t_to[d]}, device_id_type=MESH)
        for d in range(1, nt)]
    for copy in rs_copies:
        copy.start()
    total = part[tme].astype(F32)
    for d in range(1, nt):
        rs_copies[d - 1].wait_recv()
        total += rs_in[d].astype(F32)
    kv_all[tme] = total.astype(BF16)

    ag_copies = [pltpu.make_async_remote_copy(
        src_ref=kv_all.at[tme], dst_ref=kv_all.at[tme], send_sem=ag_send.at[d],
        recv_sem=ag_recv.at[d], device_id={"tile": t_to[d]}, device_id_type=MESH)
        for d in range(1, nt)]
    for copy in ag_copies:
        copy.start()
    for d in range(1, nt):
        pltpu.make_async_remote_copy(
            src_ref=kv_all.at[t_from[d]], dst_ref=kv_all.at[t_from[d]], send_sem=ag_send.at[d],
            recv_sem=ag_recv.at[d], device_id={"tile": t_to[d]}, device_id_type=MESH).wait_recv()

    step = min(2 * HD, heads * HD)
    pair = step // HD
    c_copies = []
    for kind in range(2):
        slab = e_all if kind == 0 else u_all
        if kind == 1:
            for copy in u_copies:
                copy.wait_recv()
        for l in range(layers):
            unit = kind * layers + l
            lane = 2 * HD * l + kind * HD
            side = kv_all[:, :, lane:lane + HD].reshape(rows, HD)
            wide[...] = lax.dot_general(side, slab[...], (((0,), (0,)), ((), ())),
                                        preferred_element_type=F32).astype(BF16)
            big_loads[unit].wait()

            def body(j, _):
                at = pl.ds(pl.multiple_of(j * step, step), step)
                if kind == 0:
                    core = jnp.dot(wide[...], q_w[l, :, at], preferred_element_type=F32).T
                else:
                    core = lax.dot_general(o_w[l, at, :], wide[...], (((1,), (1,)), ((), ())),
                                           preferred_element_type=F32)
                core = core.reshape(pair, nt, each, HD)
                to = pl.ds(pl.multiple_of(j * pair * each, pair * each), pair * each)
                for t in range(nt):
                    c_out[unit, t, to, :] = core[:, t].reshape(pair * each, HD).astype(BF16)
                return 0

            lax.fori_loop(0, heads // pair, body, 0)
            for d in range(1, nt):
                copy = pltpu.make_async_remote_copy(
                    src_ref=c_out.at[unit, t_to[d]], dst_ref=c_in.at[unit, d],
                    send_sem=c_send.at[unit, d], recv_sem=c_recv.at[unit, d],
                    device_id={"tile": t_to[d]}, device_id_type=MESH)
                copy.start()
                c_copies.append(copy)

    scale = 1.0 / math.sqrt(rows)
    for kind, out in enumerate((qk_ref, ov_ref)):
        for l in range(layers):
            unit = kind * layers + l
            total = c_out[unit, tme].astype(F32)
            for d in range(1, nt):
                c_copies[unit * (nt - 1) + d - 1].wait_recv()
                total += c_in[unit, d].astype(F32)
            out[l] = (total * scale).reshape(heads, each, HD)
    for copy in e_copies + u_copies + rs_copies + ag_copies + c_copies:
        copy.wait_send()


def local(nv, nt, embed, unembed, q_weight, k_weight, v_weight, o_weight, offsets):
    layers, depth, width = q_weight.shape
    heads, rows, each = width // HD, nv * SLAB_DEV, HD // nt
    chunk, units = rows // nt, 2 * layers
    out = jax.ShapeDtypeStruct((layers, heads, each, HD), F32)
    anywhere = pl.BlockSpec(memory_space=pl.ANY)
    vmem, dma = pltpu.VMEM, pltpu.SemaphoreType.DMA
    return pl.pallas_call(
        functools.partial(kernel, nv, nt, layers, heads),
        out_shape=(out, out),
        in_specs=[pl.BlockSpec(memory_space=pltpu.SMEM)] + [anywhere] * 6,
        out_specs=(pl.BlockSpec(memory_space=pltpu.VMEM),) * 2,
        scratch_shapes=[
            vmem(embed.shape, BF16), vmem(embed.shape, BF16),
            vmem((rows, depth), BF16), vmem((rows, depth), BF16),
            vmem((layers, depth, width), BF16), vmem((layers, width, depth), BF16),
            vmem((layers, depth, 2 * HD), BF16),
            vmem((nt, chunk, 2 * HD * layers), BF16), vmem((nt, chunk, 2 * HD * layers), BF16),
            vmem((nt, chunk, 2 * HD * layers), BF16),
            vmem((HD, depth), BF16),
            vmem((units, nt, heads * each, HD), BF16), vmem((units, nt, heads * each, HD), BF16),
            dma((2,)), dma((4 * layers,)), dma((nv,)), dma((nv,)), dma((nv,)), dma((nv,)),
            dma((nt,)), dma((nt,)), dma((nt,)), dma((nt,)), dma((units, nt)), dma((units, nt)),
        ],
        compiler_params=pltpu.CompilerParams(
            collective_id=0, has_side_effects=True, vmem_limit_bytes=61 * 2**20),
    )(offsets, embed, unembed, q_weight, k_weight, v_weight, o_weight)


def solution(mesh):
    return jax.shard_map(
        functools.partial(local, mesh.shape["vocab"], mesh.shape["tile"]),
        mesh=mesh,
        in_specs=(
            P("vocab", "tile"),
            P("vocab", "tile"),
            P(None, "tile", "vocab"),
            P(None, "tile", None),
            P(None, "tile", None),
            P(None, "vocab", "tile"),
            P("grp"),
        ),
        out_specs=(P("grp", "vocab", "tile", None), P("grp", "vocab", "tile", None)),
        check_vma=False,
    )
```

time: 144 us -> 59.2 us (0.41); the launches traced: 141 us -> 59 us
  waiting for transfers between devices: 101 us -> 0 us
  Pallas kernels: 0 us -> 54.4 us
  matrix products: 17.6 us -> 0 us
  between operations: 14.5 us -> 1.29 us
  other arithmetic: 3.26 us -> 0 us
  local copies, waits for them, and re-layouts: 5.1 us -> 3.34 us
    pallas_call x0 -> x1, Pallas kernels: none -> 54.4 us  [local(): pl.pallas_call(functools.partial(kernel, nv, nt, layers, heads), out_shap...]
    all_gather x2 -> x0, waiting for transfers between devices: 34.4 us -> none  [the longest x1 20.3 us: local(): all_e = lax.all_gather(slab_e, 'vocab', axis=0, tiled=True)]
    reduce_scatter x2 -> x0, waiting for transfers between devices: 34.3 us -> none  [finish(): mine = lax.psum_scatter(part, 'tile', scatter_dimension=0, tiled=True)]
    psum x1 -> x0, waiting for transfers between devices: 31.9 us -> none  [local(): k_side, v_side = lax.psum((k_part, v_part), 'tile')]
    dot_general x4 -> x0, matrix products: 17.6 us -> none  [the longest x1 6.85 us: local(): jnp.einsum('lrd,lcd->lrc', o_weight, v_wide, preferred_element_type=f32)]
    convert_element_type x2 -> x0, other arithmetic: 3.26 us -> none  [finish(): return mine.reshape(layers, heads, rows_each, HD).astype(f32)]
    unnamed x4 -> x2, local copies, waits for them, and re-layouts: 0.31 us -> 3.34 us
    dynamic_slice x2 -> x0, local copies, waits for them, and re-layouts: 2.51 us -> none  [the longest x1 1.74 us: local(): slab_u = lax.dynamic_slice_in_dim(unembed, start_row, SLAB_DEV, 0)]
  transfers between devices with their start and end apart: 5 -> 0, of which waited for: 5 -> 0; matrix products, arithmetic and copies ran while one was open for 13% -> 0% of each run, Pallas kernels for 0% -> 0%
where the time goes in v2:
time: 59.2 us; the launch traced here: 59 us
  Pallas kernels  54.4 us (92%)
  local copies, waits for them, and re-layouts  3.34 us (6%)
  between operations  1.29 us (2%)
    pallas_call x1, Pallas kernels, local(): pl.pallas_call(functools.partial(kernel, nv, nt, layers, heads), out_shap...  54.4 us
    unnamed x2, local copies, waits for them, and re-layouts  3.34 us

profile of v2, /device:TPU:1, one launch (start us, length us, event | category | flops | bytes accessed | tf_op | source)
XLA Modules:
  0.0 59.0 jit_solution(12954212901464288090)
XLA Ops:
  1.3 54.4 %shard_map.86 = (f32[2,8,32,128]{3,2,1,0:T(8,128)}, f32[2,8,32,128]{3,2,1,0:T(8,128)}) custom-call(s32[1]{0:T(128)S(6)} %copy.11.off_ref, bf16[128,2048]{1,0:T(8,128)(2,1)} %e_hbm.1, bf16[128,2048]{1,0:T(8,128)(2,1)} %u_hbm.1, bf16[2,2048,1024]{2,1,0:T(8,128)(2,1)} %q_hbm.1, bf16[2,2048,512]{2,1,0:T(8,128)(2,1)} %k_hbm.1, bf16[2,2048,512]{2,1,0:T(8,128)(2,1)} %v_hbm.1, ...), custom_call_target="tpu_custom_call" | custom-call | tf_op jit(solution)/shard_map/pallas_call | solution.py:170
  55.7 1.7 %copy.12 = f32[2,8,32,128]{3,2,1,0:T(8,128)} copy(f32[2,8,32,128]{3,2,1,0:T(8,128)} %get-tuple-element.4) | data formatting | bytes 524288
  57.3 1.7 %copy.13 = f32[2,8,32,128]{3,2,1,0:T(8,128)} copy(f32[2,8,32,128]{3,2,1,0:T(8,128)} %get-tuple-element.5) | data formatting | bytes 524288

commit v3 on v2

v3 whole, which is shorter than its diff:
```python
import functools
import math

import jax
import jax.numpy as jnp
from jax import lax
from jax.experimental import pallas as pl
from jax.experimental.pallas import tpu as pltpu
from jax.sharding import PartitionSpec as P

HD = 128
GROUP = 8
SLAB_DEV = 64
MESH = pl.DeviceIdType.MESH
BF16, F32 = jnp.bfloat16, jnp.float32


def kernel(nv, nt, layers, heads, off_ref, e_hbm, u_hbm, q_hbm, k_hbm, v_hbm, o_hbm,
           ov_ref, qk_ref, e_raw, u_raw, e_all, u_all, q_w, o_w, kv_w, part, rs_in, kv_all,
           wide, c_out, c_mid, c_sum, c_in, raw_sem, w_sem, e_send, e_recv, u_send, u_recv,
           rs_send, rs_recv, ag_send, ag_recv, m_send, m_recv, c_send, c_recv):
    vme, tme = lax.axis_index("vocab"), lax.axis_index("tile")
    chips, half = nv // 2, nt // 2
    core = lax.rem(vme, 2)
    sibling = vme + 1 - 2 * core
    chip_to = [lax.rem(vme + 2 * d, nv) for d in range(chips)]
    parity, place = lax.rem(tme, 2), tme // 2
    other = 1 - parity
    mate = tme + 1 - 2 * parity
    place_to = [lax.rem(place + d, half) for d in range(half)]
    t_to = [lax.rem(tme + d, nt) for d in range(nt)]
    t_from = [lax.rem(tme + nt - d, nt) for d in range(nt)]
    depth = e_raw.shape[1]
    rows = nv * SLAB_DEV
    chunk = rows // nt
    each = HD // nt

    barrier = pltpu.get_barrier_semaphore()
    for v in [sibling] + chip_to[1:]:
        pl.semaphore_signal(barrier, inc=1, device_id={"vocab": v}, device_id_type=MESH)
    for d in range(1, nt):
        pl.semaphore_signal(barrier, inc=1, device_id={"tile": t_to[d]}, device_id_type=MESH)

    raw = [pltpu.make_async_copy(e_hbm, e_raw, raw_sem.at[0]),
           pltpu.make_async_copy(u_hbm, u_raw, raw_sem.at[1])]
    for copy in raw:
        copy.start()
    start = pl.multiple_of(vme * heads // GROUP * HD, HD)
    kv_loads = []
    for l in range(layers):
        for kind, src in enumerate((k_hbm, v_hbm)):
            kv_loads.append(pltpu.make_async_copy(
                src.at[l, :, pl.ds(start, HD)],
                kv_w.at[l, :, pl.ds(kind * HD, HD)], w_sem.at[2 * l + kind]))
    big_loads = []
    for kind, (src, dst) in enumerate(((q_hbm, q_w), (o_hbm, o_w))):
        for l in range(layers):
            big_loads.append(pltpu.make_async_copy(
                src.at[l], dst.at[l], w_sem.at[2 * layers + kind * layers + l]))

    off = off_ref[0]
    row = lax.broadcasted_iota(jnp.int32, (SLAB_DEV, e_raw.shape[0]), 0)
    col = lax.broadcasted_iota(jnp.int32, (SLAB_DEV, e_raw.shape[0]), 1)
    pick = jnp.where(col == row + off, 1.0, 0.0).astype(BF16)
    raw[0].wait()
    e_all[:SLAB_DEV] = jnp.dot(pick, e_raw[...], preferred_element_type=F32).astype(BF16)
    raw[1].wait()
    u_all[:SLAB_DEV] = jnp.dot(pick, u_raw[...], preferred_element_type=F32).astype(BF16)
    for copy in kv_loads + big_loads:
        copy.start()

    pl.semaphore_wait(barrier, chips + nt - 1)

    def to_vocab(buf, src, dst, v, send, recv):
        return pltpu.make_async_remote_copy(
            src_ref=buf.at[pl.ds(src * SLAB_DEV, SLAB_DEV)],
            dst_ref=buf.at[pl.ds(dst * SLAB_DEV, SLAB_DEV)],
            send_sem=send.at[dst], recv_sem=recv.at[dst],
            device_id={"vocab": v}, device_id_type=MESH)

    def gather(buf, send, recv):
        across = [to_vocab(buf, 0, 2 * d, chip_to[d], send, recv) for d in range(1, chips)]
        beside = [to_vocab(buf, 2 * d, 2 * d + 1, sibling, send, recv) for d in range(chips)]
        return across, beside

    def forward(across, beside):
        for d in range(1, chips):
            across[d - 1].wait_recv()
            beside[d].start()

    e_across, e_beside = gather(e_all, e_send, e_recv)
    u_across, u_beside = gather(u_all, u_send, u_recv)
    for copy in e_across + e_beside[:1] + u_across + u_beside[:1]:
        copy.start()

    for copy in kv_loads:
        copy.wait()
    forward(e_across, e_beside)
    for copy in e_beside:
        copy.wait_recv()

    rs_copies, ag_copies = [], []
    for kind in range(2):
        for l in range(layers):
            got = jnp.dot(e_all[...], kv_w[l, :, kind * HD:(kind + 1) * HD],
                          preferred_element_type=F32).astype(BF16)
            for t in range(nt):
                part[kind, t, :, HD * l:HD * (l + 1)] = got[t * chunk:(t + 1) * chunk]
        rs_copies.append([pltpu.make_async_remote_copy(
            src_ref=part.at[kind, t_to[d]], dst_ref=rs_in.at[kind, d],
            send_sem=rs_send.at[kind, d], recv_sem=rs_recv.at[kind, d],
            device_id={"tile": t_to[d]}, device_id_type=MESH) for d in range(1, nt)])
        for copy in rs_copies[kind]:
            copy.start()
    for kind in range(2):
        total = part[kind, tme].astype(F32)
        for d in range(1, nt):
            rs_copies[kind][d - 1].wait_recv()
            total += rs_in[kind, d].astype(F32)
        kv_all[kind, tme] = total.astype(BF16)
        ag_copies.append([pltpu.make_async_remote_copy(
            src_ref=kv_all.at[kind, tme], dst_ref=kv_all.at[kind, tme],
            send_sem=ag_send.at[kind, d], recv_sem=ag_recv.at[kind, d],
            device_id={"tile": t_to[d]}, device_id_type=MESH) for d in range(1, nt)])
        for copy in ag_copies[kind]:
            copy.start()
    forward(u_across, u_beside)

    step = min(2 * HD, heads * HD)
    pair = step // HD
    m_copies, c_copies = [], []

    def second(unit):
        m_copies[unit].wait_recv()
        copies = []
        for d in range(1, half):
            k = place_to[d]
            c_sum[unit, d] = (c_out[unit, parity, k].astype(F32)
                              + c_mid[unit, k].astype(F32)).astype(BF16)
            copies.append(pltpu.make_async_remote_copy(
                src_ref=c_sum.at[unit, d], dst_ref=c_in.at[unit, d],
                send_sem=c_send.at[unit, d], recv_sem=c_recv.at[unit, d],
                device_id={"tile": 2 * k + parity}, device_id_type=MESH))
            copies[-1].start()
        c_copies.append(copies)

    for kind in range(2):
        slab = e_all if kind == 0 else u_all
        for d in range(1, nt):
            at = kv_all.at[kind, t_from[d]]
            pltpu.make_async_remote_copy(
                src_ref=at, dst_ref=at, send_sem=ag_send.at[kind, d],
                recv_sem=ag_recv.at[kind, d], device_id={"tile": t_to[d]},
                device_id_type=MESH).wait_recv()
        if kind == 1:
            for copy in u_beside:
                copy.wait_recv()
        for l in range(layers):
            unit = kind * layers + l
            side = kv_all[kind, :, :, HD * l:HD * (l + 1)].reshape(rows, HD)
            wide[...] = lax.dot_general(side, slab[...], (((0,), (0,)), ((), ())),
                                        preferred_element_type=F32).astype(BF16)
            big_loads[unit].wait()

            def body(j, _):
                at = pl.ds(pl.multiple_of(j * step, step), step)
                if kind == 0:
                    cores = jnp.dot(wide[...], q_w[l, :, at], preferred_element_type=F32).T
                else:
                    cores = lax.dot_general(o_w[l, at, :], wide[...], (((1,), (1,)), ((), ())),
                                            preferred_element_type=F32)
                cores = cores.reshape(pair, nt, each, HD)
                to = pl.ds(pl.multiple_of(j * pair * each, pair * each), pair * each)
                for t in range(nt):
                    c_out[unit, t % 2, t // 2, to, :] = cores[:, t].reshape(pair * each, HD).astype(BF16)
                return 0

            lax.fori_loop(0, heads // pair, body, 0)
            m_copies.append(pltpu.make_async_remote_copy(
                src_ref=c_out.at[unit, other], dst_ref=c_mid.at[unit],
                send_sem=m_send.at[unit], recv_sem=m_recv.at[unit],
                device_id={"tile": mate}, device_id_type=MESH))
            m_copies[unit].start()
            if unit > 0:
                second(unit - 1)
    second(2 * layers - 1)

    scale = 1.0 / math.sqrt(rows)
    for kind, out in enumerate((qk_ref, ov_ref)):
        for l in range(layers):
            unit = kind * layers + l
            total = c_out[unit, parity, place].astype(F32) + c_mid[unit, place].astype(F32)
            for d in range(1, half):
                c_copies[unit][d - 1].wait_recv()
                total += c_in[unit, d].astype(F32)
            out[l] = (total * scale).reshape(heads, each, HD)
    for copies in [e_across, e_beside, u_across, u_beside, m_copies] + rs_copies + ag_copies + c_copies:
        for copy in copies:
            copy.wait_send()


def local(nv, nt, embed, unembed, q_weight, k_weight, v_weight, o_weight, offsets):
    layers, depth, width = q_weight.shape
    heads, rows, each = width // HD, nv * SLAB_DEV, HD // nt
    chunk, units = rows // nt, 2 * layers
    out = jax.ShapeDtypeStruct((layers, heads, each, HD), F32)
    anywhere = pl.BlockSpec(memory_space=pl.ANY)
    vmem, dma = pltpu.VMEM, pltpu.SemaphoreType.DMA
    return pl.pallas_call(
        functools.partial(kernel, nv, nt, layers, heads),
        out_shape=(out, out),
        in_specs=[pl.BlockSpec(memory_space=pltpu.SMEM)] + [anywhere] * 6,
        out_specs=(pl.BlockSpec(memory_space=pltpu.VMEM),) * 2,
        scratch_shapes=[
            vmem(embed.shape, BF16), vmem(embed.shape, BF16),
            vmem((rows, depth), BF16), vmem((rows, depth), BF16),
            vmem((layers, depth, width), BF16), vmem((layers, width, depth), BF16),
            vmem((layers, depth, 2 * HD), BF16),
            vmem((2, nt, chunk, HD * layers), BF16), vmem((2, nt, chunk, HD * layers), BF16),
            vmem((2, nt, chunk, HD * layers), BF16),
            vmem((HD, depth), BF16),
            vmem((units, 2, nt // 2, heads * each, HD), BF16),
            vmem((units, nt // 2, heads * each, HD), BF16),
            vmem((units, nt // 2, heads * each, HD), BF16),
            vmem((units, nt // 2, heads * each, HD), BF16),
            dma((2,)), dma((4 * layers,)), dma((nv,)), dma((nv,)), dma((nv,)), dma((nv,)),
            dma((2, nt)), dma((2, nt)), dma((2, nt)), dma((2, nt)),
            dma((units,)), dma((units,)), dma((units, nt // 2)), dma((units, nt // 2)),
        ],
        compiler_params=pltpu.CompilerParams(
            collective_id=0, has_side_effects=True, vmem_limit_bytes=61 * 2**20),
    )(offsets, embed, unembed, q_weight, k_weight, v_weight, o_weight)


def solution(mesh):
    return jax.shard_map(
        functools.partial(local, mesh.shape["vocab"], mesh.shape["tile"]),
        mesh=mesh,
        in_specs=(
            P("vocab", "tile"),
            P("vocab", "tile"),
            P(None, "tile", "vocab"),
            P(None, "tile", None),
            P(None, "tile", None),
            P(None, "vocab", "tile"),
            P("grp"),
        ),
        out_specs=(P("grp", "vocab", "tile", None), P("grp", "vocab", "tile", None)),
        check_vma=False,
    )
```

time: 59.2 us -> 55 us (0.929)
  Pallas kernels: 54.4 us -> 50.1 us
    pallas_call x1, Pallas kernels: 54.4 us -> 50.1 us  [local(): pl.pallas_call(functools.partial(kernel, nv, nt, layers, heads), out_shap...]
where the time goes in v3:
time: 55 us; the launch traced here: 54.7 us
  Pallas kernels  50.1 us (91%)
  local copies, waits for them, and re-layouts  3.34 us (6%)
  between operations  1.29 us (2%)
    pallas_call x1, Pallas kernels, local(): pl.pallas_call(functools.partial(kernel, nv, nt, layers, heads), out_shap...  50.1 us
    unnamed x2, local copies, waits for them, and re-layouts  3.34 us

profile of v3, /device:TPU:1, one launch (start us, length us, event | category | flops | bytes accessed | tf_op | source)
XLA Modules:
  0.0 54.7 jit_solution(5985107904520193229)
XLA Ops:
  1.3 50.1 %shard_map.86 = (f32[2,8,32,128]{3,2,1,0:T(8,128)}, f32[2,8,32,128]{3,2,1,0:T(8,128)}) custom-call(s32[1]{0:T(128)S(6)} %copy.11.off_ref, bf16[128,2048]{1,0:T(8,128)(2,1)} %e_hbm.1, bf16[128,2048]{1,0:T(8,128)(2,1)} %u_hbm.1, bf16[2,2048,1024]{2,1,0:T(8,128)(2,1)} %q_hbm.1, bf16[2,2048,512]{2,1,0:T(8,128)(2,1)} %k_hbm.1, bf16[2,2048,512]{2,1,0:T(8,128)(2,1)} %v_hbm.1, ...), custom_call_target="tpu_custom_call" | custom-call | tf_op jit(solution)/shard_map/pallas_call | solution.py:209
  51.3 1.7 %copy.12 = f32[2,8,32,128]{3,2,1,0:T(8,128)} copy(f32[2,8,32,128]{3,2,1,0:T(8,128)} %get-tuple-element.4) | data formatting | bytes 524288
  53.0 1.7 %copy.13 = f32[2,8,32,128]{3,2,1,0:T(8,128)} copy(f32[2,8,32,128]{3,2,1,0:T(8,128)} %get-tuple-element.5) | data formatting | bytes 524288

commit v4 on v3

--- a/solution.py
+++ b/solution.py
@@ -16,7 +16,7 @@
 
 
 def kernel(nv, nt, layers, heads, off_ref, e_hbm, u_hbm, q_hbm, k_hbm, v_hbm, o_hbm,
-           ov_ref, qk_ref, e_raw, u_raw, e_all, u_all, q_w, o_w, kv_w, part, rs_in, kv_all,
+           out_ref, e_raw, u_raw, e_all, u_all, q_w, o_w, kv_w, part, rs_in, kv_all,
            wide, c_out, c_mid, c_sum, c_in, raw_sem, w_sem, e_send, e_recv, u_send, u_recv,
            rs_send, rs_recv, ag_send, ag_recv, m_send, m_recv, c_send, c_recv):
     vme, tme = lax.axis_index("vocab"), lax.axis_index("tile")
@@ -90,12 +90,14 @@
 
     e_across, e_beside = gather(e_all, e_send, e_recv)
     u_across, u_beside = gather(u_all, u_send, u_recv)
-    for copy in e_across + e_beside[:1] + u_across + u_beside[:1]:
+    for copy in e_across + e_beside[:1]:
         copy.start()
 
     for copy in kv_loads:
         copy.wait()
     forward(e_across, e_beside)
+    for copy in u_across + u_beside[:1]:
+        copy.start()
     for copy in e_beside:
         copy.wait_recv()
 
@@ -185,15 +187,14 @@
                 second(unit - 1)
     second(2 * layers - 1)
 
-    scale = 1.0 / math.sqrt(rows)
-    for kind, out in enumerate((qk_ref, ov_ref)):
+    for kind in range(2):
         for l in range(layers):
             unit = kind * layers + l
             total = c_out[unit, parity, place].astype(F32) + c_mid[unit, place].astype(F32)
             for d in range(1, half):
                 c_copies[unit][d - 1].wait_recv()
                 total += c_in[unit, d].astype(F32)
-            out[l] = (total * scale).reshape(heads, each, HD)
+            out_ref[1 - kind, l] = total.reshape(heads, each, HD)
     for copies in [e_across, e_beside, u_across, u_beside, m_copies] + rs_copies + ag_copies + c_copies:
         for copy in copies:
             copy.wait_send()
@@ -203,14 +204,14 @@
     layers, depth, width = q_weight.shape
     heads, rows, each = width // HD, nv * SLAB_DEV, HD // nt
     chunk, units = rows // nt, 2 * layers
-    out = jax.ShapeDtypeStruct((layers, heads, each, HD), F32)
+    out = jax.ShapeDtypeStruct((2, layers, heads, each, HD), F32)
     anywhere = pl.BlockSpec(memory_space=pl.ANY)
     vmem, dma = pltpu.VMEM, pltpu.SemaphoreType.DMA
-    return pl.pallas_call(
+    cores = pl.pallas_call(
         functools.partial(kernel, nv, nt, layers, heads),
-        out_shape=(out, out),
+        out_shape=out,
         in_specs=[pl.BlockSpec(memory_space=pltpu.SMEM)] + [anywhere] * 6,
-        out_specs=(pl.BlockSpec(memory_space=pltpu.VMEM),) * 2,
+        out_specs=pl.BlockSpec(memory_space=pltpu.VMEM),
         scratch_shapes=[
             vmem(embed.shape, BF16), vmem(embed.shape, BF16),
             vmem((rows, depth), BF16), vmem((rows, depth), BF16),
@@ -230,6 +231,8 @@
         compiler_params=pltpu.CompilerParams(
             collective_id=0, has_side_effects=True, vmem_limit_bytes=61 * 2**20),
     )(offsets, embed, unembed, q_weight, k_weight, v_weight, o_weight)
+    scale = 1.0 / math.sqrt(rows)
+    return cores[0] * scale, cores[1] * scale
 
 
 def solution(mesh):

time: 55 us -> 52.9 us (0.962)
  local copies, waits for them, and re-layouts: 3.34 us -> 0 us
  other arithmetic: 0 us -> 1.86 us
  Pallas kernels: 50.1 us -> 49.2 us
    unnamed x2 -> x0, local copies, waits for them, and re-layouts: 3.34 us -> none
    mul x0 -> x1, other arithmetic: none -> 1.86 us  [local(): return (cores[0] * scale, cores[1] * scale)]
    pallas_call x1, Pallas kernels: 50.1 us -> 49.2 us  [local(): pl.pallas_call(functools.partial(kernel, nv, nt, layers, heads), out_shap...]
where the time goes in v4:
time: 52.9 us; the launch traced here: 52.3 us
  Pallas kernels  49.2 us (93%)
  other arithmetic  1.86 us (4%)
  between operations  1.29 us (2%)
    pallas_call x1, Pallas kernels, local(): pl.pallas_call(functools.partial(kernel, nv, nt, layers, heads), out_shap...  49.2 us
    mul x1, other arithmetic, local(): return (cores[0] * scale, cores[1] * scale)  1.86 us

profile of v4, /device:TPU:1, one launch (start us, length us, event | category | flops | bytes accessed | tf_op | source)
XLA Modules:
  0.0 52.3 jit_solution(17849253213056515639)
XLA Ops:
  1.3 49.2 %shard_map.86 = f32[2,2,8,32,128]{4,3,2,1,0:T(8,128)} custom-call(s32[1]{0:T(128)S(6)} %copy.9.off_ref, bf16[128,2048]{1,0:T(8,128)(2,1)} %e_hbm.1, bf16[128,2048]{1,0:T(8,128)(2,1)} %u_hbm.1, bf16[2,2048,1024]{2,1,0:T(8,128)(2,1)} %q_hbm.1, bf16[2,2048,512]{2,1,0:T(8,128)(2,1)} %k_hbm.1, bf16[2,2048,512]{2,1,0:T(8,128)(2,1)} %v_hbm.1, ...), custom_call_target="tpu_custom_call" | custom-call | tf_op jit(solution)/shard_map/pallas_call | solution.py:210
  50.5 1.9 %multiply_bitcast_fusion = (f32[2,8,32,128]{3,2,1,0:T(8,128)}, f32[2,8,32,128]{3,2,1,0:T(8,128)}) fusion(f32[2,2,8,32,128]{4,3,2,1,0:T(8,128)} %shard_map.86), kind=kLoop, calls=%fused_computation | loop fusion | flops 131072 | bytes 1048576 | tf_op jit(solution)/shard_map/mul | solution.py:235

commit v5 on v4

--- a/solution.py
+++ b/solution.py
@@ -128,7 +128,7 @@
             copy.start()
     forward(u_across, u_beside)
 
-    step = min(2 * HD, heads * HD)
+    step = min(4 * HD, heads * HD)
     pair = step // HD
     m_copies, c_copies = [], []
 
@@ -177,7 +177,7 @@
                     c_out[unit, t % 2, t // 2, to, :] = cores[:, t].reshape(pair * each, HD).astype(BF16)
                 return 0
 
-            lax.fori_loop(0, heads // pair, body, 0)
+            lax.fori_loop(0, heads // pair, body, 0, unroll=True)
             m_copies.append(pltpu.make_async_remote_copy(
                 src_ref=c_out.at[unit, other], dst_ref=c_mid.at[unit],
                 send_sem=m_send.at[unit], recv_sem=m_recv.at[unit],

time: 52.9 us -> 53.4 us (level)
  Pallas kernels: 49.2 us -> 49.8 us
    pallas_call x1, Pallas kernels: 49.2 us -> 49.8 us  [local(): pl.pallas_call(functools.partial(kernel, nv, nt, layers, heads), out_shap...]
where the time goes in v5:
time: 53.4 us; the launch traced here: 52.9 us
  Pallas kernels  49.8 us (93%)
  other arithmetic  1.86 us (3%)
  between operations  1.29 us (2%)
    pallas_call x1, Pallas kernels, local(): pl.pallas_call(functools.partial(kernel, nv, nt, layers, heads), out_shap...  49.8 us
    mul x1, other arithmetic, local(): return (cores[0] * scale, cores[1] * scale)  1.86 us

profile of v5, /device:TPU:1, one launch (start us, length us, event | category | flops | bytes accessed | tf_op | source)
XLA Modules:
  0.0 52.9 jit_solution(2051790112506685392)
XLA Ops:
  1.3 49.8 %shard_map.86 = f32[2,2,8,32,128]{4,3,2,1,0:T(8,128)} custom-call(s32[1]{0:T(128)S(6)} %copy.9.off_ref, bf16[128,2048]{1,0:T(8,128)(2,1)} %e_hbm.1, bf16[128,2048]{1,0:T(8,128)(2,1)} %u_hbm.1, bf16[2,2048,1024]{2,1,0:T(8,128)(2,1)} %q_hbm.1, bf16[2,2048,512]{2,1,0:T(8,128)(2,1)} %k_hbm.1, bf16[2,2048,512]{2,1,0:T(8,128)(2,1)} %v_hbm.1, ...), custom_call_target="tpu_custom_call" | custom-call | tf_op jit(solution)/shard_map/pallas_call | solution.py:210
  51.0 1.9 %multiply_bitcast_fusion = (f32[2,8,32,128]{3,2,1,0:T(8,128)}, f32[2,8,32,128]{3,2,1,0:T(8,128)}) fusion(f32[2,2,8,32,128]{4,3,2,1,0:T(8,128)} %shard_map.86), kind=kLoop, calls=%fused_computation | loop fusion | flops 131072 | bytes 1048576 | tf_op jit(solution)/shard_map/mul | solution.py:235

commit v6 on v4

--- a/solution.py
+++ b/solution.py
@@ -17,8 +17,9 @@
 
 def kernel(nv, nt, layers, heads, off_ref, e_hbm, u_hbm, q_hbm, k_hbm, v_hbm, o_hbm,
            out_ref, e_raw, u_raw, e_all, u_all, q_w, o_w, kv_w, part, rs_in, kv_all,
-           wide, c_out, c_mid, c_sum, c_in, raw_sem, w_sem, e_send, e_recv, u_send, u_recv,
-           rs_send, rs_recv, ag_send, ag_recv, m_send, m_recv, c_send, c_recv):
+           wide, c_out, c_mid, c_sum, c_in, c_dir, raw_sem, w_sem, e_send, e_recv, u_send, u_recv,
+           rs_send, rs_recv, ag_send, ag_recv, m_send, m_recv, c_send, c_recv,
+           d_send, d_recv):
     vme, tme = lax.axis_index("vocab"), lax.axis_index("tile")
     chips, half = nv // 2, nt // 2
     core = lax.rem(vme, 2)
@@ -130,7 +131,7 @@
 
     step = min(2 * HD, heads * HD)
     pair = step // HD
-    m_copies, c_copies = [], []
+    m_copies, c_copies, last = [], [], 2 * layers - 1
 
     def second(unit):
         m_copies[unit].wait_recv()
@@ -178,6 +179,15 @@
                 return 0
 
             lax.fori_loop(0, heads // pair, body, 0)
+            if unit == last:
+                second(unit - 1)
+                d_copies = [pltpu.make_async_remote_copy(
+                    src_ref=c_out.at[unit, lax.rem(t_to[d], 2), t_to[d] // 2],
+                    dst_ref=c_dir.at[d], send_sem=d_send.at[d], recv_sem=d_recv.at[d],
+                    device_id={"tile": t_to[d]}, device_id_type=MESH) for d in range(1, nt)]
+                for copy in d_copies:
+                    copy.start()
+                continue
             m_copies.append(pltpu.make_async_remote_copy(
                 src_ref=c_out.at[unit, other], dst_ref=c_mid.at[unit],
                 send_sem=m_send.at[unit], recv_sem=m_recv.at[unit],
@@ -185,17 +195,22 @@
             m_copies[unit].start()
             if unit > 0:
                 second(unit - 1)
-    second(2 * layers - 1)
 
     for kind in range(2):
         for l in range(layers):
             unit = kind * layers + l
-            total = c_out[unit, parity, place].astype(F32) + c_mid[unit, place].astype(F32)
-            for d in range(1, half):
-                c_copies[unit][d - 1].wait_recv()
-                total += c_in[unit, d].astype(F32)
+            total = c_out[unit, parity, place].astype(F32)
+            if unit == last:
+                for d in range(1, nt):
+                    d_copies[d - 1].wait_recv()
+                    total += c_dir[d].astype(F32)
+            else:
+                total += c_mid[unit, place].astype(F32)
+                for d in range(1, half):
+                    c_copies[unit][d - 1].wait_recv()
+                    total += c_in[unit, d].astype(F32)
             out_ref[1 - kind, l] = total.reshape(heads, each, HD)
-    for copies in [e_across, e_beside, u_across, u_beside, m_copies] + rs_copies + ag_copies + c_copies:
+    for copies in [e_across, e_beside, u_across, u_beside, m_copies, d_copies] + rs_copies + ag_copies + c_copies:
         for copy in copies:
             copy.wait_send()
 
@@ -224,9 +239,11 @@
             vmem((units, nt // 2, heads * each, HD), BF16),
             vmem((units, nt // 2, heads * each, HD), BF16),
             vmem((units, nt // 2, heads * each, HD), BF16),
+            vmem((nt, heads * each, HD), BF16),
             dma((2,)), dma((4 * layers,)), dma((nv,)), dma((nv,)), dma((nv,)), dma((nv,)),
             dma((2, nt)), dma((2, nt)), dma((2, nt)), dma((2, nt)),
             dma((units,)), dma((units,)), dma((units, nt // 2)), dma((units, nt // 2)),
+            dma((nt,)), dma((nt,)),
         ],
         compiler_params=pltpu.CompilerParams(
             collective_id=0, has_side_effects=True, vmem_limit_bytes=61 * 2**20),

time: 52.9 us -> 54.4 us (1.028)
  the two profiles are of different devices: /device:TPU:1 before, /device:TPU:0 now
where the time goes in v6:
time: 54.4 us; the launch traced here: 54.2 us
  Pallas kernels  51 us (94%)
  other arithmetic  1.86 us (3%)
  between operations  1.29 us (2%)
    pallas_call x1, Pallas kernels, local(): pl.pallas_call(functools.partial(kernel, nv, nt, layers, heads), out_shap...  51 us
    mul x1, other arithmetic, local(): return (cores[0] * scale, cores[1] * scale)  1.86 us

profile of v6, /device:TPU:0, one launch (start us, length us, event | category | flops | bytes accessed | tf_op | source)
XLA Modules:
  0.0 54.2 jit_solution(13064163027808634686)
XLA Ops:
  1.3 51.0 %shard_map.86 = f32[2,2,8,32,128]{4,3,2,1,0:T(8,128)} custom-call(s32[1]{0:T(128)S(6)} %copy.9.off_ref, bf16[128,2048]{1,0:T(8,128)(2,1)} %e_hbm.1, bf16[128,2048]{1,0:T(8,128)(2,1)} %u_hbm.1, bf16[2,2048,1024]{2,1,0:T(8,128)(2,1)} %q_hbm.1, bf16[2,2048,512]{2,1,0:T(8,128)(2,1)} %k_hbm.1, bf16[2,2048,512]{2,1,0:T(8,128)(2,1)} %v_hbm.1, ...), custom_call_target="tpu_custom_call" | custom-call | tf_op jit(solution)/shard_map/pallas_call | solution.py:225
  52.3 1.9 %multiply_bitcast_fusion = (f32[2,8,32,128]{3,2,1,0:T(8,128)}, f32[2,8,32,128]{3,2,1,0:T(8,128)}) fusion(f32[2,2,8,32,128]{4,3,2,1,0:T(8,128)} %shard_map.86), kind=kLoop, calls=%fused_computation | loop fusion | flops 131072 | bytes 1048576 | tf_op jit(solution)/shard_map/mul | solution.py:252

commit v7 on v4

--- a/solution.py
+++ b/solution.py
@@ -58,16 +58,15 @@
             big_loads.append(pltpu.make_async_copy(
                 src.at[l], dst.at[l], w_sem.at[2 * layers + kind * layers + l]))
 
+    for copy in kv_loads:
+        copy.start()
+
     off = off_ref[0]
     row = lax.broadcasted_iota(jnp.int32, (SLAB_DEV, e_raw.shape[0]), 0)
     col = lax.broadcasted_iota(jnp.int32, (SLAB_DEV, e_raw.shape[0]), 1)
     pick = jnp.where(col == row + off, 1.0, 0.0).astype(BF16)
     raw[0].wait()
     e_all[:SLAB_DEV] = jnp.dot(pick, e_raw[...], preferred_element_type=F32).astype(BF16)
-    raw[1].wait()
-    u_all[:SLAB_DEV] = jnp.dot(pick, u_raw[...], preferred_element_type=F32).astype(BF16)
-    for copy in kv_loads + big_loads:
-        copy.start()
 
     pl.semaphore_wait(barrier, chips + nt - 1)
 
@@ -90,8 +89,10 @@
 
     e_across, e_beside = gather(e_all, e_send, e_recv)
     u_across, u_beside = gather(u_all, u_send, u_recv)
-    for copy in e_across + e_beside[:1]:
-        copy.start()
+    for copy in e_across + e_beside[:1] + big_loads:
+        copy.start()
+    raw[1].wait()
+    u_all[:SLAB_DEV] = jnp.dot(pick, u_raw[...], preferred_element_type=F32).astype(BF16)
 
     for copy in kv_loads:
         copy.wait()

time: 52.9 us -> 52.7 us (level)
  no operation moved by 1% of the time
where the time goes in v7:
time: 52.7 us; the launch traced here: 52.5 us
  Pallas kernels  49.4 us (94%)
  other arithmetic  1.86 us (4%)
  between operations  1.29 us (2%)
    pallas_call x1, Pallas kernels, local(): pl.pallas_call(functools.partial(kernel, nv, nt, layers, heads), out_shap...  49.4 us
    mul x1, other arithmetic, local(): return (cores[0] * scale, cores[1] * scale)  1.86 us

profile of v7, /device:TPU:1, one launch (start us, length us, event | category | flops | bytes accessed | tf_op | source)
XLA Modules:
  0.0 52.5 jit_solution(5554852803839542237)
XLA Ops:
  1.3 49.4 %shard_map.86 = f32[2,2,8,32,128]{4,3,2,1,0:T(8,128)} custom-call(s32[1]{0:T(128)S(6)} %copy.9.off_ref, bf16[128,2048]{1,0:T(8,128)(2,1)} %e_hbm.1, bf16[128,2048]{1,0:T(8,128)(2,1)} %u_hbm.1, bf16[2,2048,1024]{2,1,0:T(8,128)(2,1)} %q_hbm.1, bf16[2,2048,512]{2,1,0:T(8,128)(2,1)} %k_hbm.1, bf16[2,2048,512]{2,1,0:T(8,128)(2,1)} %v_hbm.1, ...), custom_call_target="tpu_custom_call" | custom-call | tf_op jit(solution)/shard_map/pallas_call | solution.py:211
  50.6 1.9 %multiply_bitcast_fusion = (f32[2,8,32,128]{3,2,1,0:T(8,128)}, f32[2,8,32,128]{3,2,1,0:T(8,128)}) fusion(f32[2,2,8,32,128]{4,3,2,1,0:T(8,128)} %shard_map.86), kind=kLoop, calls=%fused_computation | loop fusion | flops 131072 | bytes 1048576 | tf_op jit(solution)/shard_map/mul | solution.py:236
